TPU v7x, 256 devices: a whole 4x4x8 slice. The times are simulated.
256 devices in a mesh: pre: 2 (over x_lo), dec: 64 (over z, y, core), rep: 2 (over x_hi).
Axes of the slice: x: 4 (x_hi: 2, x_lo: 2; x = x_hi * 2 + x_lo), y: 4, z: 8, core: 2. Of those that a mesh axis runs over, the one named last changes fastest.
Arguments:
- queries: bfloat16 [4096, 128, 576], P('dec', ('pre', 'rep')), may hold values from -170 to 170
- prefix_of: int32 [4096, 1], P('dec'), may hold values from 0 to 63; in each aligned block of 64 rows (0 to 63, 64 to 127, ...) at most 2 rows name the same one
- prefix_cache: bfloat16 [64, 1024, 576], P('dec'), may hold values from -6 to 6
- suffix_cache: bfloat16 [4096, 32, 576], P('dec'), may hold values from -6 to 6
- suffix_len: int32 [4096], P('dec'), may hold values from 1 to 32
- fresh_pages: bfloat16 [4096, 64, 576], P('dec', ('pre', 'rep')), may hold values from -6 to 6
- page_owner: int32 [4096, 1], replicated, may hold values from 0 to 63; in each aligned block of 64 rows (0 to 63, 64 to 127, ...) at most 2 rows name the same one
- page_request: int32 [4096], replicated, may hold values from 0 to 63
- page_tokens: int32 [4096], replicated, may hold values from 1 to 64
- value_up: bfloat16 [128, 512, 128], P(('pre', 'rep')), may hold values from -0.25 to 0.25
Outputs:
- attn_out: bfloat16 [4096, 16384], P('dec', ('pre', 'rep'))
Inputs may be any that keep to these rules, and one draw needn't show every extreme that they name: `prefix_of`: among the 64 requests of one index of dec (aligned blocks of rows), no prefix is named more than 2 times. `page_owner`: among the 64 fresh pages of one index of dec (aligned blocks of rows), no owner is named more than 2 times.
All inputs are finite; a program needn't handle non-finite values.
Results may differ from a plain program's by a relative error of at most 0.011.
Values may be sent and summed in bfloat16 or wider, within the bound.
A program may use at most 256 MiB of HBM per device.

v0:
```python
import jax
import jax.numpy as jnp
from jax import lax
from jax.sharding import PartitionSpec as P

DL = 512


softmax_scale = 192.0 ** (-0.5)
neg_fill = -1e30


def block_partial(queried, key_rows, allowed):
    scores = (
        jnp.einsum("brd,btd->brt", queried, key_rows, preferred_element_type=jnp.float32)
        * softmax_scale
    )
    scores = jnp.where(allowed, scores, neg_fill)
    maxima = jnp.max(scores, axis=-1)
    weights = jnp.exp(scores - maxima[..., None]).astype(jnp.bfloat16)
    totals = jnp.sum(weights.astype(jnp.float32), axis=-1)
    summed = jnp.einsum(
        "brt,btd->brd", weights, key_rows[..., :DL], preferred_element_type=jnp.float32
    )
    return (summed, maxima, totals)


def bucket_slots(targets, capacity):
    length = targets.shape[0]
    same_target = targets[:, None] == targets[None, :]
    earlier = jnp.arange(length)[None, :] < jnp.arange(length)[:, None]
    before = jnp.sum((same_target & earlier).astype(jnp.int32), axis=1)
    return targets * capacity + before


def project(latent, value_up):
    latent_high = latent.astype(jnp.bfloat16)
    latent_low = (latent - latent_high.astype(jnp.float32)).astype(jnp.bfloat16)
    high_part = jnp.einsum(
        "rhd,hde->rhe", latent_high, value_up, preferred_element_type=jnp.float32
    )
    low_part = jnp.einsum("rhd,hde->rhe", latent_low, value_up, preferred_element_type=jnp.float32)
    return high_part + low_part


def per_device(
    queries,
    prefix_of,
    prefix_cache,
    suffix_cache,
    suffix_len,
    fresh_pages,
    page_owner,
    page_request,
    page_tokens,
    value_up,
):
    row_count = queries.shape[0]
    head_count = queries.shape[1]
    feature_width = queries.shape[2]
    owner_count = lax.axis_size("dec")
    capacity = 2 * row_count // owner_count
    slot_count = owner_count * capacity
    my_index = lax.axis_index("dec")
    suffix_span = suffix_cache.shape[1]
    resident_ok = jnp.arange(suffix_span)[None, None, :] < suffix_len[:, None, None]
    resident_sum, resident_max, resident_total = block_partial(queries, suffix_cache, resident_ok)
    query_slot = bucket_slots(prefix_of[:, 0], capacity)
    query_buffer = (
        jnp.zeros((slot_count, head_count, feature_width), jnp.bfloat16).at[query_slot].set(queries)
    )
    query_buffer = query_buffer.reshape(owner_count, capacity, head_count, feature_width)
    arrived = lax.all_to_all(query_buffer, "dec", split_axis=0, concat_axis=0, tiled=True)
    sources = arrived.shape[0]
    slots_here = arrived.shape[1]
    flat_rows = arrived.reshape(1, sources * slots_here * head_count, feature_width)
    summed, maxima, totals = block_partial(flat_rows, prefix_cache, True)
    summed = summed.reshape(sources * slots_here, head_count, DL)
    out_width = summed.shape[-1]
    prefix_sum = lax.all_to_all(
        summed.reshape(sources, slots_here, head_count, out_width),
        "dec",
        split_axis=0,
        concat_axis=0,
        tiled=True,
    ).reshape(slot_count, head_count, -1)[query_slot]
    prefix_max = lax.all_to_all(
        maxima.reshape(sources, slots_here, head_count),
        "dec",
        split_axis=0,
        concat_axis=0,
        tiled=True,
    ).reshape(slot_count, head_count)[query_slot]
    prefix_total = lax.all_to_all(
        totals.reshape(sources, slots_here, head_count),
        "dec",
        split_axis=0,
        concat_axis=0,
        tiled=True,
    ).reshape(slot_count, head_count)[query_slot]
    split_rows = fresh_pages.shape[1]
    all_owner = page_owner[:, 0].reshape(owner_count, row_count)
    my_owner = lax.dynamic_index_in_dim(all_owner, my_index, 0, keepdims=False)
    send_slot = bucket_slots(my_owner, capacity)
    send_buffer = (
        jnp.zeros((slot_count, split_rows, feature_width), jnp.bfloat16)
        .at[send_slot]
        .set(fresh_pages)
    )
    send_buffer = send_buffer.reshape(owner_count, capacity, split_rows, feature_width)
    arrived_pages = lax.all_to_all(send_buffer, "dec", split_axis=0, concat_axis=0, tiled=True)
    whole_pages = lax.all_gather(arrived_pages, ("pre", "rep"), axis=2, tiled=True)
    whole_pages = whole_pages.reshape(slot_count, -1, feature_width)
    all_slot = jax.vmap(bucket_slots, in_axes=(0, None))(all_owner, capacity)
    wanted = my_index * capacity + jnp.arange(capacity)
    matched = (all_slot[:, None, :] == wanted[None, :, None]).astype(jnp.int32)
    alive = (jnp.sum(matched, axis=2) > 0).reshape(-1)
    page_req = jnp.sum(matched * page_request.reshape(owner_count, 1, row_count), axis=2).reshape(
        -1
    )
    page_len = jnp.sum(matched * page_tokens.reshape(owner_count, 1, row_count), axis=2).reshape(-1)
    page_span = whole_pages.shape[1]
    page_ok = jnp.arange(page_span)[None, None, :] < page_len[:, None, None]
    page_sum, page_max, page_total = block_partial(queries[page_req], whole_pages, page_ok)
    member = (page_req[:, None] == jnp.arange(row_count)[None, :]) & alive[:, None]
    fresh_best = jnp.max(jnp.where(member[:, :, None], page_max[:, None, :], neg_fill), axis=0)
    highest = jnp.maximum(jnp.maximum(prefix_max, resident_max), fresh_best)
    prefix_coef = jnp.exp(prefix_max - highest)
    resident_coef = jnp.exp(resident_max - highest)
    page_coef = jnp.exp(page_max - highest[page_req]) * alive[:, None].astype(jnp.float32)
    member_f = member.astype(jnp.float32)
    denominator = (
        prefix_coef * prefix_total
        + resident_coef * resident_total
        + jnp.einsum("sr,sh->rh", member_f, page_coef * page_total, precision=lax.Precision.HIGHEST)
    )
    remainder = resident_coef[..., None] * resident_sum + jnp.einsum(
        "sr,shd->rhd", member_f, page_coef[..., None] * page_sum, precision=lax.Precision.HIGHEST
    )
    latent_out = (prefix_coef[..., None] * prefix_sum + remainder) / denominator[..., None]
    mixed = project(latent_out, value_up)
    return mixed.astype(jnp.bfloat16).reshape(row_count, -1)


def solution(mesh):
    placed = (
        P("dec", ("pre", "rep"), None),
        P("dec", None),
        P("dec", None, None),
        P("dec", None, None),
        P("dec"),
        P("dec", ("pre", "rep"), None),
        P(),
        P(),
        P(),
        P(("pre", "rep"), None, None),
    )
    return jax.shard_map(
        per_device, mesh=mesh, in_specs=placed, out_specs=P("dec", ("pre", "rep")), check_vma=False
    )
```

profile of v0, /device:TPU:32, one launch (start us, length us, event | category | flops | bytes accessed | tf_op | source)
XLA Modules:
  0.0 489.7 jit_solution(194294664178964899)
XLA Ops:
  9.0 6.3 %scatter_fusion.1 = bf16[128,16,576]{2,1,0:T(8,128)(2,1)S(1)} fusion(bf16[128,16,576]{2,1,0:T(8,128)(2,1)S(1)} %broadcast_in_dim.48, s32[64]{0:T(128)S(1)} %fusion.37, bf16[64,16,576]{2,1,0:T(8,128)(2,1)} %param.15), kind=kCustom, calls=%fused_computation.6 | custom fusion | bytes 3539200 | tf_op jit(solution)/shard_map/scatter | solution.py:108
  16.8 12.1 %all-to-all-start.2 = ((bf16[64,2,16,576]{3,2,1,0:T(8,128)(2,1)}), bf16[64,2,16,576]{3,2,1,0:T(8,128)(2,1)}, u32[]{:S(2)}, u32[]{:S(2)}) async-start(bf16[64,2,16,576]{3,2,1,0:T(8,128)(2,1)} %bitcast.61), calls=%async_computation.2 | async-start | bytes 5242880 | tf_op jit(solution)/shard_map/all_to_all | solution.py:111
  29.1 2.7 broadcast_in_dim.43
  31.8 9.1 %scatter_fusion = bf16[128,32,576]{2,1,0:T(8,128)(2,1)} fusion(bf16[128,32,576]{2,1,0:T(8,128)(2,1)} %broadcast_in_dim.43, s32[64]{0:T(128)S(1)} %fusion.35, bf16[64,32,576]{2,1,0:T(8,128)(2,1)S(1)} %copy-done), kind=kCustom, calls=%fused_computation.5 | custom fusion | bytes 7078144 | tf_op jit(solution)/shard_map/scatter | solution.py:70
  40.9 49.5 %all-to-all-done.2 = bf16[64,2,16,576]{3,2,1,0:T(8,128)(2,1)} async-done(((bf16[64,2,16,576]{3,2,1,0:T(8,128)(2,1)}), bf16[64,2,16,576]{3,2,1,0:T(8,128)(2,1)}, u32[]{:S(2)}, u32[]{:S(2)}) %all-to-all-start.2) | async-done | bytes 2359328 | tf_op jit(solution)/shard_map/all_to_all | solution.py:111
  90.5 6.5 %all-to-all-start = ((bf16[64,2,32,576]{3,2,1,0:T(8,128)(2,1)}), bf16[64,2,32,576]{3,2,1,0:T(8,128)(2,1)}, u32[]{:S(2)}, u32[]{:S(2)}) async-start(bf16[64,2,32,576]{3,2,1,0:T(8,128)(2,1)} %bitcast.60), calls=%async_computation | async-start | bytes 10485760 | tf_op jit(solution)/shard_map/all_to_all | solution.py:73
  97.8 117.1 %all-to-all-done = bf16[64,2,32,576]{3,2,1,0:T(8,128)(2,1)} async-done(((bf16[64,2,32,576]{3,2,1,0:T(8,128)(2,1)}), bf16[64,2,32,576]{3,2,1,0:T(8,128)(2,1)}, u32[]{:S(2)}, u32[]{:S(2)}) %all-to-all-start) | async-done | bytes 4718624 | tf_op jit(solution)/shard_map/all_to_all | solution.py:73
  214.8 12.2 %multiply_reduce_fusion = (f32[4096]{0:T(1024)S(1)}, f32[4096,1024]{1,0:T(8,128)}) fusion(bf16[4096,576]{1,0:T(8,128)(2,1)} %bitcast.4, bf16[1,1024,576]{1,2,0:T(8,128)(2,1)} %param.12), kind=kOutput, calls=%fused_computation.9 | convolution fusion | flops 4840222720 | bytes 22691840 | tf_op jit(solution)/shard_map/brd,btd->brt/dot_general | solution.py:15
  227.8 6.4 %all-to-all-start.1 = ((f32[64,2,32]{2,1,0:T(2,128)}), f32[64,2,32]{2,1,0:T(2,128)S(1)}, u32[]{:S(2)}, u32[]{:S(2)}) async-start(f32[64,2,32]{2,1,0:T(2,128)} %reshape.295), calls=%async_computation.1 | async-start | bytes 131072 | tf_op jit(solution)/shard_map/all_to_all | solution.py:87
  234.2 10.3 %convert_reduce_fusion = (f32[4096]{0:T(1024)S(1)}, bf16[4096,1024]{1,0:T(8,128)(2,1)}) fusion(f32[4096]{0:T(1024)S(1)} %get-tuple-element.16, f32[4096,1024]{1,0:T(8,128)} %get-tuple-element.17), kind=kLoop, calls=%fused_computation.7 | loop fusion | flops 20967424 | bytes 25198592 | tf_op jit(solution)/shard_map/reduce_sum | solution.py:21
  245.3 10.3 %all-to-all-start.4 = ((f32[64,2,32]{2,1,0:T(2,128)}), f32[64,2,32]{2,1,0:T(2,128)S(1)}, u32[]{:S(2)}, u32[]{:S(2)}) async-start(f32[64,2,32]{2,1,0:T(2,128)} %reshape.302), calls=%async_computation.4 | async-start | bytes 131072 | tf_op jit(solution)/shard_map/all_to_all | solution.py:94
  255.6 11.5 %fusion.26 = f32[64,2,32,512]{3,2,1,0:T(8,128)} fusion(bf16[64,2,32,1024]{3,2,1,0:T(8,128)(2,1)} %bitcast.62, bf16[1,1024,576]{1,2,0:T(8,128)(2,1)} %param.12), kind=kOutput, calls=%fused_computation.37 | convolution fusion | flops 4294967296 | bytes 17825792 | tf_op jit(solution)/shard_map/brt,btd->brd/dot_general | solution.py:22
  267.1 10.6 %all-to-all-start.3 = ((f32[64,2,32,512]{3,2,1,0:T(8,128)}), f32[64,2,32,512]{3,2,1,0:T(8,128)}, u32[]{:S(2)}, u32[]{:S(2)}) async-start(f32[64,2,32,512]{3,2,1,0:T(8,128)} %fusion.26), calls=%async_computation.3 | async-start | bytes 16777216 | tf_op jit(solution)/shard_map/all_to_all | solution.py:80
  277.9 1.9 convert_reduce_fusion.2
  280.5 3.5 gather_fusion.1
  284.6 3.7 fusion.41
  291.4 9.0 %fusion.13 = (f32[128,32]{1,0:T(8,128)S(1)}, f32[128,32,64]{2,1,0:T(8,128)S(1)}) fusion(pred[128,64]{1,0:T(8,128)(4,1)S(1)} %iota_compare_fusion, bf16[128,32,576]{2,1,0:T(8,128)(2,1)} %gather_fusion.1, bf16[128,64,576]{2,1,0:T(8,128)(2,1)} %bitcast.58), kind=kOutput, calls=%fused_computation.28 | convolution fusion | flops 302772224 | bytes 15228928 | tf_op jit(solution)/shard_map/brd,btd->brt/dot_general | solution.py:15
  303.5 5.1 %broadcast_multiply_fusion = f32[128,32,512]{2,1,0:T(8,128)S(1)} fusion(f32[128,32]{1,0:T(8,128)S(1)} %exponential_multiply_fusion, bf16[128,64,576]{2,1,0:T(8,128)(2,1)} %bitcast.59, f32[128,32,64]{2,1,0:T(8,128)S(1)} %get-tuple-element.15, f32[128,32]{1,0:T(8,128)S(1)} %get-tuple-element.14, pred[128,64]{1,0:T(8,128)(4,1)S(1)} %iota_compare_fusion), kind=kOutput, calls=%fused_computation.18 | convolution fusion | flops 271581184 | bytes 17866752 | tf_op jit(solution)/shard_map/brt,btd->brd/dot_general | solution.py:22
  308.7 8.1 %fusion.2 = f32[64,32,512]{2,0,1:T(8,128)} fusion(f32[128,32,512]{2,1,0:T(8,128)S(1)} %broadcast_multiply_fusion, s32[128]{0:T(128)S(1)} %eq.85, pred[128]{0:T(512)(128)(4,1)S(1)} %gt.21), kind=kOutput, calls=%fused_computation.12 | convolution fusion | flops 1610629120 | bytes 12583552 | tf_op jit(solution)/shard_map/sr,shd->rhd/dot_general | solution.py:137
  316.8 147.2 %all-to-all-done.3 = f32[64,2,32,512]{3,2,1,0:T(8,128)} async-done(((f32[64,2,32,512]{3,2,1,0:T(8,128)}), f32[64,2,32,512]{3,2,1,0:T(8,128)}, u32[]{:S(2)}, u32[]{:S(2)}) %all-to-all-start.3) | async-done | bytes 8388640 | tf_op jit(solution)/shard_map/all_to_all | solution.py:80
  464.0 6.2 %gather_fusion.2 = f32[64,32,512]{2,1,0:T(8,128)} fusion(f32[128,32,512]{2,1,0:T(8,128)} %bitcast.18, s32[1024]{0:T(1024)S(1)} %pad_clamp_fusion.1), kind=kCustom, calls=%fused_computation.2 | custom fusion | bytes 8388864 | tf_op jit(solution)/shard_map/gather | solution.py:80
  470.2 6.7 %subtract_convert_fusion = (bf16[64,32,512]{2,1,0:T(8,128)(2,1)S(1)}, bf16[64,32,512]{2,1,0:T(8,128)(2,1)S(1)}) fusion(f32[64,32]{1,0:T(8,128)S(1)} %copy.79, f32[64,32,512]{2,0,1:T(8,128)} %fusion.2, bf16[64,32,576]{2,1,0:T(8,128)(2,1)} %param.13, f32[64,32,32]{1,2,0:T(8,128)S(1)} %copy-done.3, f32[64,32]{1,0:T(8,128)S(1)} %get-tuple-element.18, ...), kind=kOutput, calls=%fused_computation.17 | convolution fusion | flops 76677120 | bytes 14974976 | tf_op jit(solution)/shard_map/brt,btd->brd/dot_general | solution.py:22
  476.9 2.5 fusion.8
  479.4 2.6 fusion.21
  (74 shorter events, 14.8 us)
Async XLA Ops:
  8.9 19.9 %copy-start.7 = (s32[64,1]{0,1:T(1,128)S(1)}, s32[64,1]{0,1:T(1,128)}, u32[]{:S(2)}) copy-start(s32[64,1]{0,1:T(1,128)} %param.11) | copy-start | bytes 772
  15.3 1.5 copy-start.2
  16.8 15.0 %copy-start = (bf16[64,32,576]{2,1,0:T(8,128)(2,1)S(1)}, bf16[64,32,576]{2,1,0:T(8,128)(2,1)}, u32[]{:S(2)}) copy-start(bf16[64,32,576]{2,1,0:T(8,128)(2,1)} %param.10) | copy-start | bytes 7077892
  16.8 73.6 %all-to-all-start.2 = ((bf16[64,2,16,576]{3,2,1,0:T(8,128)(2,1)}), bf16[64,2,16,576]{3,2,1,0:T(8,128)(2,1)}, u32[]{:S(2)}, u32[]{:S(2)}) async-start(bf16[64,2,16,576]{3,2,1,0:T(8,128)(2,1)} %bitcast.61), calls=%async_computation.2 | async-start | bytes 5242880 | tf_op jit(solution)/shard_map/all_to_all | solution.py:111
  90.5 124.4 %all-to-all-start = ((bf16[64,2,32,576]{3,2,1,0:T(8,128)(2,1)}), bf16[64,2,32,576]{3,2,1,0:T(8,128)(2,1)}, u32[]{:S(2)}, u32[]{:S(2)}) async-start(bf16[64,2,32,576]{3,2,1,0:T(8,128)(2,1)} %bitcast.60), calls=%async_computation | async-start | bytes 10485760 | tf_op jit(solution)/shard_map/all_to_all | solution.py:73
  97.0 194.4 %all-gather.2.cloned.1.call-start = ((), (), s32[]{:S(2)}) async-start(), calls=%async_computation.5 | async-start | bytes 13107200 | tf_op jit(solution)/shard_map/all_gather | solution.py:112
  227.8 17.4 %all-to-all-start.1 = ((f32[64,2,32]{2,1,0:T(2,128)}), f32[64,2,32]{2,1,0:T(2,128)S(1)}, u32[]{:S(2)}, u32[]{:S(2)}) async-start(f32[64,2,32]{2,1,0:T(2,128)} %reshape.295), calls=%async_computation.1 | async-start | bytes 131072 | tf_op jit(solution)/shard_map/all_to_all | solution.py:87
  245.3 21.8 %all-to-all-start.4 = ((f32[64,2,32]{2,1,0:T(2,128)}), f32[64,2,32]{2,1,0:T(2,128)S(1)}, u32[]{:S(2)}, u32[]{:S(2)}) async-start(f32[64,2,32]{2,1,0:T(2,128)} %reshape.302), calls=%async_computation.4 | async-start | bytes 131072 | tf_op jit(solution)/shard_map/all_to_all | solution.py:94
  267.1 10.7 %copy-start.4 = (s32[4096]{0:T(1024)S(1)}, s32[4096]{0:T(1024)}, u32[]{:S(2)}) copy-start(s32[4096]{0:T(1024)} %param.17) | copy-start | bytes 49156
  267.1 10.7 %copy-start.5 = (s32[4096]{0:T(1024)S(1)}, s32[4096]{0:T(1024)}, u32[]{:S(2)}) copy-start(s32[4096]{0:T(1024)} %param.18) | copy-start | bytes 49156
  267.1 196.9 %all-to-all-start.3 = ((f32[64,2,32,512]{3,2,1,0:T(8,128)}), f32[64,2,32,512]{3,2,1,0:T(8,128)}, u32[]{:S(2)}, u32[]{:S(2)}) async-start(f32[64,2,32,512]{3,2,1,0:T(8,128)} %fusion.26), calls=%async_computation.3 | async-start | bytes 16777216 | tf_op jit(solution)/shard_map/all_to_all | solution.py:80
  280.5 4.0 copy-start.6
  464.0 6.2 %copy-start.3 = (f32[64,32,32]{1,2,0:T(8,128)S(1)}, f32[64,32,32]{1,2,0:T(8,128)}, u32[]{:S(2)}) copy-start(f32[64,32,32]{1,2,0:T(8,128)} %get-tuple-element.19) | copy-start | bytes 786436
  470.2 6.7 %copy-start.1 = (bf16[32,512,128]{2,1,0:T(8,128)(2,1)S(1)}, bf16[32,512,128]{2,1,0:T(8,128)(2,1)}, u32[]{:S(2)}) copy-start(bf16[32,512,128]{2,1,0:T(8,128)(2,1)} %param.19) | copy-start | bytes 12582916
Sparse Core Ops, SparseCore 0:
  99.7 188.5 all-gather.1
where the time goes:
time: 491 us; the launch traced here: 490 us
  waiting for transfers between devices  315 us (64%)
  matrix products  61.6 us (13%)
  starting transfers between devices  46 us (9%)
  local copies, waits for them, and re-layouts  36.2 us (7%)
  other arithmetic  17.7 us (4%)
  between operations  13.7 us (3%)
    all_to_all x1, waiting for transfers between devices, per_device(): lax.all_to_all(summed.reshape(sources, slots_here, head_count, out_width)...  147 us
    all_to_all x1, waiting for transfers between devices, per_device(): lax.all_to_all(query_buffer, 'dec', split_axis=0, concat_axis=0, tiled=True)  117 us
    all_to_all x1, waiting for transfers between devices, per_device(): lax.all_to_all(send_buffer, 'dec', split_axis=0, concat_axis=0, tiled=True)  49.5 us
    dot_general x3, matrix products, block_partial(): jnp.einsum('brd,btd->brt', queried, key_rows, preferred_element_type=jnp....  24.9 us
    dot_general x3, matrix products, block_partial(): jnp.einsum('brt,btd->brd', weights, key_rows[..., :DL], preferred_element...  23.3 us
    reduce_sum x3, other arithmetic, block_partial(): totals = jnp.sum(weights.astype(jnp.float32), axis=-1)  13.1 us
    all_to_all x1, starting transfers between devices, per_device(): lax.all_to_all(send_buffer, 'dec', split_axis=0, concat_axis=0, tiled=True)  12.1 us
    all_to_all x1, starting transfers between devices, per_device(): lax.all_to_all(summed.reshape(sources, slots_here, head_count, out_width)...  10.6 us
  transfers between devices with their start and end apart: 6, of which 3 were waited for; matrix products, arithmetic and copies ran while one was open for 18% of the time, Pallas kernels for 0%

commit v1 on v0

v1 whole, which is shorter than its diff:
```python
import functools

import jax
import jax.numpy as jnp
from jax import lax
from jax.experimental import pallas as pl
from jax.experimental.pallas import tpu as pltpu
from jax.sharding import PartitionSpec as P

MESH = pl.DeviceIdType.MESH
BF, F32 = jnp.bfloat16, jnp.float32
ANY = pl.BlockSpec(memory_space=pl.ANY)
VM = pl.BlockSpec(memory_space=pltpu.VMEM)
SM = pl.BlockSpec(memory_space=pltpu.SMEM)
DL, DQ = 512, 576
SCALE = 192.0**-0.5
NEG = -1e30
ORDER = (0, 1, -1, 2, -2, 3, -3, 4)
D, Q = 512, 128
PIECE = 128
DQDS = (((1, 0)), ((-1, 0)), ((1, 1)), ((-1, 1)), ((2, 0)), ((2, 1)), ((0, 1)))


def bucket_kernel(pref, owner, queries, fresh, qs, ps, slot, count):
    dec = lax.axis_index("dec")
    qs[...] = jnp.zeros_like(qs)
    ps[...] = jnp.zeros_like(ps)

    def clear(i, c):
        count[0, i] = 0
        count[1, i] = 0
        return c

    lax.fori_loop(0, 64, clear, 0, unroll=8)

    def put(i, c):
        p = pref[i]
        k = count[0, p]
        count[0, p] = k + 1
        to = (p % 8) * 16 + (p // 8) * 2 + k
        qs[to] = queries[i]
        slot[i] = to
        o = owner[dec * 64 + i]
        k = count[1, o]
        count[1, o] = k + 1
        ps[o * 2 + k] = fresh[i]
        return c

    lax.fori_loop(0, 64, put, 0)


def bucket(pref, owner, queries, fresh):
    qs, ps, slot = pl.pallas_call(
        bucket_kernel,
        out_shape=(
            jax.ShapeDtypeStruct((128, 32, DQ), BF),
            jax.ShapeDtypeStruct((128, 16, DQ), BF),
            jax.ShapeDtypeStruct((64,), jnp.int32),
        ),
        in_specs=[SM, SM, VM, VM],
        out_specs=(VM, VM, SM),
        scratch_shapes=[pltpu.SMEM((2, 64), jnp.int32)],
        compiler_params=pltpu.CompilerParams(vmem_limit_bytes=40 * 2**20),
    )(pref, owner, queries, fresh)
    return qs.reshape(8, 8, 2, 32, DQ), ps.reshape(64, 2, 16, DQ), slot


def rcopy(src, dst, ss, rs, dev):
    return pltpu.make_async_remote_copy(
        src_ref=src, dst_ref=dst, send_sem=ss, recv_sem=rs, device_id=dev, device_id_type=MESH
    )


def nt(a, b):
    return lax.dot_general(a, b, (((1,), (1,)), ((), ())), preferred_element_type=F32)


def nn(a, b):
    return jnp.dot(a, b, preferred_element_type=F32)


def exchange_kernel(
    qs, pf, ps, vu, W, ret, rlse,
    qr, pa, lat, lse, outs, lses,
    qss, qrs, rss, rrs, pss, prs, xss, xrs, yss, yrs, bss, brs, loc,
):
    pre, dec, rep = lax.axis_index("pre"), lax.axis_index("dec"), lax.axis_index("rep")
    z, y, core = dec // 8, (dec // 2) % 4, dec % 2
    yc = dec % 8
    x = rep * 2 + pre
    g = pre * 2 + rep

    def at_x(v):
        v = v % 4
        return (v % 2, dec, v // 2)

    def g_of(v):
        v = v % 4
        return (v % 2) * 2 + v // 2

    right, left = at_x(x + 1), at_x(x + 3)
    bar = pltpu.get_barrier_semaphore()

    def hello(o, c):
        pl.semaphore_signal(bar, inc=1, device_id=(pre, (dec + o) % 64, rep), device_id_type=MESH)
        return c

    lax.fori_loop(1, 64, hello, 0)
    pl.semaphore_signal(bar, inc=1, device_id=right, device_id_type=MESH)
    pl.semaphore_signal(bar, inc=1, device_id=left, device_id_type=MESH)
    pl.semaphore_wait(bar, 65)

    def start(c):
        c.start()
        return c

    own_q = start(pltpu.make_async_copy(qs.at[yc], qr.at[:, yc], loc.at[0]))
    own_p = start(pltpu.make_async_copy(pf, pa.at[z], loc.at[1]))
    own_w = start(pltpu.make_async_copy(ps.at[dec], W.at[dec, :, g], loc.at[2]))

    def peer(dy, dc):
        return ((y + dy + 4) % 4) * 2 + (core + dc) % 2

    def query_send(j, n):
        dy, dc = DQDS[n]
        t = peer(dy, dc)
        part = pl.ds(2 * j, 2)
        return start(rcopy(qs.at[t, part], qr.at[part, yc], qss.at[n], qrs.at[n], (pre, z * 8 + t, rep)))

    def query_wait(n):
        dy, dc = DQDS[n]
        s = peer(-dy, dc)
        return rcopy(qs.at[0], qr.at[:, s], qss.at[n], qrs.at[n], (pre, z * 8 + s, rep))

    def zdev(dz):
        return (pre, ((z + dz + 8) % 8) * 8 + yc, rep)

    def piece(n, last, dirn):
        if n == 0:
            return pl.ds(D + g * Q + dirn * (Q // 2), Q // 2) if last else pl.ds(D + g * Q, Q)
        return pl.ds((n - 1) * PIECE, PIECE)

    def pieces(dirn, t):
        if t < 4:
            return (0, 1, 2, 3, 4)
        return (0, 1, 2) if dirn == 0 else (0, 3, 4)

    rings = {}

    def ring_start(dirn, t, n):
        sgn = 1 - 2 * dirn
        blk = (z - sgn * (t - 1) + 8) % 8
        rows = piece(n, t == 4, dirn)
        src = pf.at[rows] if t == 1 else pa.at[blk, rows]
        rings[dirn, t, n] = start(
            rcopy(src, pa.at[blk, rows], rss.at[dirn, t - 1, n], rrs.at[dirn, t - 1, n], zdev(sgn))
        )

    def page_send(b):
        dz = ORDER[b]

        def one(o, c):
            t = ((z + dz + 8) % 8) * 8 + (yc + o) % 8
            rcopy(ps.at[t], W.at[dec, :, g], pss.at[b], prs.at[b], (pre, t, rep)).start()
            return c

        lax.fori_loop(1 if dz == 0 else 0, 8, one, 0)

    def batch(b):
        return pl.ds(((z - ORDER[b] + 8) % 8) * 8, 8)

    def page_wait(b):
        w = W.at[pl.ds(0, 7 if ORDER[b] == 0 else 8), :, 0]
        c = rcopy(w, w, pss.at[b], prs.at[b], right)
        c.wait_send()
        c.wait_recv()

    xs = {}

    def x_start(b):
        r = W.at[batch(b), :, g]
        xs[b] = [
            start(rcopy(r, r, xss.at[0, b], xrs.at[0, b], right)),
            start(rcopy(r, r, xss.at[1, b], xrs.at[1, b], left)),
        ]

    def x_forward(b):
        xs[b][0].wait_recv()
        r = W.at[batch(b), 0, g_of(x + 3)]
        xs[b].append(start(rcopy(r, r, xss.at[2, b], xrs.at[2, b], right)))
        xs[b][1].wait_recv()
        r = W.at[batch(b), 1, g_of(x + 1)]
        xs[b].append(start(rcopy(r, r, xss.at[3, b], xrs.at[3, b], left)))

    def x_end(b):
        xs[b][2].wait_recv()
        xs[b][3].wait_recv()

    ys = {}

    def y_start(blk, n):
        r = pa.at[blk, pl.ds(D + g * Q, Q)]
        ys[n] = [
            blk,
            start(rcopy(r, r, yss.at[0, n], yrs.at[0, n], right)),
            start(rcopy(r, r, yss.at[1, n], yrs.at[1, n], left)),
        ]

    def y_forward(n):
        blk = ys[n][0]
        ys[n][1].wait_recv()
        r = pa.at[blk, pl.ds(D + g_of(x + 3) * Q, Q // 2)]
        ys[n].append(start(rcopy(r, r, yss.at[2, n], yrs.at[2, n], right)))
        ys[n][2].wait_recv()
        r = pa.at[blk, pl.ds(D + g_of(x + 1) * Q + Q // 2, Q // 2)]
        ys[n].append(start(rcopy(r, r, yss.at[3, n], yrs.at[3, n], left)))

    def y_end(n):
        ys[n][3].wait_recv()
        ys[n][4].wait_recv()

    def attend(blk):
        def half(i, c):
            q = qr[blk, pl.ds(i * 4, 4)].reshape(256, DQ)
            s = nt(q, pa[blk])
            top = jnp.max(s, axis=1, keepdims=True)
            w = jnp.exp((s - top) * SCALE).astype(BF)
            total = jnp.sum(w.astype(F32), axis=1, keepdims=True)
            o = nn(w, pa[blk, :, :DL]) / total
            l = jnp.broadcast_to(top * SCALE + jnp.log(total), (256, 128))
            for n in range(4):
                at = pl.ds(pl.multiple_of((i * 4 + n) * 512 + blk * 64, 64), 64)
                for f in range(4):
                    lat[f, at, :] = o[n * 64 : n * 64 + 64, f * 128 : f * 128 + 128]
                lse[at, :] = l[n * 64 : n * 64 + 64]
            return c

        lax.fori_loop(0, 2, half, 0)

    for n in range(5):
        ring_start(0, 1, n)
        ring_start(1, 1, n)
        if n == 0:
            page_send(0)
        else:
            for m in range(7):
                query_send(n - 1, m)
    page_send(1)
    page_send(2)
    for t in range(1, 5):
        for n in range(5):
            for dirn in (0, 1):
                if n not in pieces(dirn, t):
                    continue
                rings[dirn, t, n].wait_recv()
                if t < 4 and n in pieces(dirn, t + 1):
                    ring_start(dirn, t + 1, n)
                if n == 0 and t < 4:
                    y_start((z - t + 8) % 8 if dirn == 0 else (z + t) % 8, 2 * t - 2 + dirn)
            if t == 4 and n == 0:
                y_start((z + 4) % 8, 6)
        if t < 3:
            page_send(2 * t + 1)
            page_send(2 * t + 2)
        if t == 3:
            page_send(7)
        if t > 1:
            y_forward(2 * t - 4)
            y_forward(2 * t - 3)
        if t == 1:
            own_w.wait()
            page_wait(0)
            x_start(0)
        if t == 2:
            page_wait(1)
            page_wait(2)
            x_start(1)
            x_start(2)
            x_forward(0)
        if t == 3:
            x_forward(1)
            x_forward(2)
    y_forward(6)
    page_wait(3)
    page_wait(4)
    x_start(3)
    x_start(4)
    own_q.wait()
    own_p.wait()
    for n in range(7):
        query_wait(n).wait_recv()
    attend(z)
    y_end(0)
    y_end(1)
    attend((z + 7) % 8)
    attend((z + 1) % 8)
    x_forward(3)
    x_forward(4)
    page_wait(5)
    page_wait(6)
    x_start(5)
    x_start(6)
    y_end(2)
    y_end(3)
    attend((z + 6) % 8)
    attend((z + 2) % 8)
    y_end(4)
    y_end(5)
    attend((z + 5) % 8)
    attend((z + 3) % 8)
    x_forward(5)
    x_forward(6)
    page_wait(7)
    x_start(7)
    y_end(6)
    attend((z + 4) % 8)

    lane = lax.broadcasted_iota(jnp.int32, (128, 128), 1)

    def project(h, c):
        rows = pl.ds(h, 128, stride=32)
        latent = jnp.concatenate([lat[f, rows, :] for f in range(4)], axis=1)
        outs[h] = nn(latent.astype(BF), vu[h]).astype(BF)
        return jnp.where(lane == h, lse[rows, :], c)

    lses[...] = lax.fori_loop(0, 32, project, jnp.zeros((128, 128), F32))

    back = []
    for n in range(7):
        dy, dc = DQDS[n]
        t = peer(dy, dc)
        there, here = pl.ds(t * 16, 16), pl.ds(yc * 16, 16)
        dev = (pre, z * 8 + t, rep)
        back.append(start(rcopy(outs.at[:, there], ret.at[:, here], bss.at[0, n], brs.at[0, n], dev)))
        back.append(start(rcopy(lses.at[there], rlse.at[here], bss.at[1, n], brs.at[1, n], dev)))
    here = pl.ds(yc * 16, 16)
    mine = [
        start(pltpu.make_async_copy(outs.at[:, here], ret.at[:, here], loc.at[3])),
        start(pltpu.make_async_copy(lses.at[here], rlse.at[here], loc.at[4])),
    ]
    x_forward(7)

    for b in range(8):
        x_end(b)
    for c in back:
        c.wait()
    for c in mine:
        c.wait()
    for n in range(7):
        query_wait(n).wait_send()
        for c in ys[n][1:]:
            c.wait_send()
    for c in rings.values():
        c.wait_send()
    for b in range(8):
        for c in xs[b]:
            c.wait_send()


def exchange(qs, pf, ps, vu):
    S = pltpu.SemaphoreType.DMA
    return pl.pallas_call(
        exchange_kernel,
        out_shape=(
            jax.ShapeDtypeStruct((64, 2, 4, 16, DQ), BF),
            jax.ShapeDtypeStruct((32, 128, 128), BF),
            jax.ShapeDtypeStruct((128, 128), F32),
        ),
        in_specs=[ANY, ANY, ANY, VM],
        out_specs=(ANY, ANY, ANY),
        scratch_shapes=[
            pltpu.VMEM((8, 8, 2, 32, DQ), BF),
            pltpu.VMEM((8, 1024, DQ), BF),
            pltpu.VMEM((4, 4096, 128), F32),
            pltpu.VMEM((4096, 128), F32),
            pltpu.VMEM((32, 128, 128), BF),
            pltpu.VMEM((128, 128), F32),
            S((7,)), S((7,)), S((2, 4, 5)), S((2, 4, 5)), S((8,)), S((8,)),
            S((4, 8)), S((4, 8)), S((4, 7)), S((4, 7)), S((2, 7)), S((2, 7)), S((5,)),
        ],
        compiler_params=pltpu.CompilerParams(
            collective_id=0, has_side_effects=True, vmem_limit_bytes=56 * 2**20
        ),
    )(qs, pf, ps, vu)


def local_kernel(
    req, length, q, suffix, slen, pages, vu, slot, ret, rlse, out, acc, top, tot
):
    step = pl.program_id(0)

    @pl.when(step == 0)
    def _():
        acc[...] = jnp.zeros_like(acc)
        tot[...] = jnp.zeros_like(tot)
        top[...] = jnp.full_like(top, NEG)

    def merge(r, m, l, o):
        at = pl.ds(pl.multiple_of(r * 32, 32), 32)
        old = top[at, :1]
        new = jnp.maximum(old, m)
        a, b = jnp.exp(old - new), jnp.exp(m - new)
        for f in range(4):
            acc[f, at, :] = acc[f, at, :] * a + o[:, f * 128 : f * 128 + 128] * b
        tot[at, :] = tot[at, :] * a + l * b
        top[at, :] = jnp.broadcast_to(new, (32, 128))

    def block(queried, keys, span, lens, count):
        rows, cols = count * 32, count * span
        r = lax.broadcasted_iota(jnp.int32, (rows, 1), 0) // 32
        limit = jnp.zeros((rows, 1), jnp.int32)
        for n in range(count):
            limit = jnp.where(r == n, lens[n], limit)
        c = lax.broadcasted_iota(jnp.int32, (rows, cols), 1) - r * span
        ok = (c >= 0) & (c < limit)
        s = jnp.where(ok, nt(queried, keys) * SCALE, NEG)
        m = jnp.max(s, axis=1, keepdims=True)
        w = jnp.where(ok, jnp.exp(s - m), 0.0).astype(BF)
        l = jnp.sum(w.astype(F32), axis=1, keepdims=True)
        return m, l, nn(w, keys[:, :DL])

    first = step * 8
    queried = q[pl.ds(first, 8)].reshape(256, DQ)
    m, l, o = block(queried, suffix[...].reshape(256, DQ), 32, [slen[first + n] for n in range(8)], 8)
    for n in range(8):
        at = slice(n * 32, n * 32 + 32)
        merge(first + n, m[at], l[at], o[at])

    for k in range(4):
        s0 = step * 16 + k * 4
        owners = [req[s0 + n] for n in range(4)]
        queried = jnp.concatenate([q[r] for r in owners], axis=0)
        keys = pages[k * 4 : k * 4 + 4].reshape(256, DQ)
        m, l, o = block(queried, keys, 64, [length[s0 + n] for n in range(4)], 4)
        for n in range(4):
            at = slice(n * 32, n * 32 + 32)
            merge(owners[n], m[at], l[at], o[at])

    @pl.when(step == pl.num_programs(0) - 1)
    def _():
        hot = lax.broadcasted_iota(jnp.int32, (64, 128), 1) == slot[...]
        pick = hot.astype(BF)
        plse = jnp.dot(hot.astype(F32), rlse[...], precision=lax.Precision.HIGHEST, preferred_element_type=F32)
        lane = lax.broadcasted_iota(jnp.int32, (64, 128), 1)

        def head(h, c):
            rows = pl.ds(h, 64, stride=32)
            lsep = jnp.sum(jnp.where(lane == h, plse, 0.0), axis=1, keepdims=True)
            total = tot[rows, :][:, :1]
            lser = top[rows, :][:, :1] + jnp.log(total)
            high = jnp.maximum(lsep, lser)
            ep, er = jnp.exp(lsep - high), jnp.exp(lser - high)
            latent = jnp.concatenate([acc[f, rows, :] for f in range(4)], axis=1)
            here = nn((latent / total).astype(BF), vu[h])
            there = nn(pick, ret[h])
            out[:, pl.ds(pl.multiple_of(h * 128, 128), 128)] = ((ep * there + er * here) / (ep + er)).astype(BF)
            return c

        lax.fori_loop(0, 32, head, 0, unroll=4)


def local(req, length, q, suffix, slen, pages, vu, slot, ret, rlse):
    def whole(shape):
        return pl.BlockSpec(shape, lambda *a: (0,) * len(shape))

    return pl.pallas_call(
        local_kernel,
        grid=(8,),
        out_shape=jax.ShapeDtypeStruct((64, 4096), BF),
        in_specs=[
            SM, SM,
            whole((64, 32, DQ)),
            pl.BlockSpec((8, 32, DQ), lambda i: (i, 0, 0)),
            SM,
            pl.BlockSpec((16, 64, DQ), lambda i: (i, 0, 0)),
            whole((32, DL, 128)),
            whole((64, 1)),
            whole((32, 128, 128)),
            whole((128, 128)),
        ],
        out_specs=whole((64, 4096)),
        scratch_shapes=[
            pltpu.VMEM((4, 2048, 128), F32),
            pltpu.VMEM((2048, 128), F32),
            pltpu.VMEM((2048, 128), F32),
        ],
        compiler_params=pltpu.CompilerParams(vmem_limit_bytes=56 * 2**20),
    )(req, length, q, suffix, slen, pages, vu, slot, ret, rlse)


def per_device(
    queries, prefix_of, prefix_cache, suffix_cache, suffix_len, fresh_pages,
    page_owner, page_request, page_tokens, value_up,
):
    dec = lax.axis_index("dec")
    qs, ps, slot = bucket(prefix_of[:, 0], page_owner[:, 0], queries, fresh_pages)
    W, ret, rlse = exchange(qs, prefix_cache[0], ps, value_up)

    mine = page_owner[:, 0].reshape(64, 64) == dec
    nth = jnp.cumsum(mine.astype(jnp.int32), axis=1)
    pick = mine[:, None, :] & (nth[:, None, :] == jnp.arange(1, 3)[None, :, None])
    req = jnp.sum(jnp.where(pick, page_request.reshape(64, 1, 64), 0), axis=2).reshape(128)
    length = jnp.sum(jnp.where(pick, page_tokens.reshape(64, 1, 64), 0), axis=2).reshape(128)
    return local(
        req, length, queries, suffix_cache, suffix_len, W.reshape(128, 64, DQ), value_up,
        slot.reshape(64, 1), ret, rlse,
    )


def solution(mesh):
    heads = ("pre", "rep")
    placed = (
        P("dec", heads, None),
        P("dec", None),
        P("dec", None, None),
        P("dec", None, None),
        P("dec"),
        P("dec", heads, None),
        P(),
        P(),
        P(),
        P(heads, None, None),
    )
    return jax.shard_map(
        per_device, mesh=mesh, in_specs=placed, out_specs=P("dec", heads), check_vma=False
    )
```

time: 491 us -> 247 us (0.50)
  waiting for transfers between devices: 315 us -> 0 us
  Pallas kernels: 0 us -> 230 us
  matrix products: 61.6 us -> 0 us
  starting transfers between devices: 46 us -> 0 us
  local copies, waits for them, and re-layouts: 36.2 us -> 12.2 us
  other arithmetic: 17.7 us -> 0.51 us
  between operations: 13.7 us -> 0.06 us
    all_to_all x5 -> x0, waiting for transfers between devices: 314 us -> none  [the longest x1 147 us: per_device(): lax.all_to_all(summed.reshape(sources, slots_here, head_count, out_width)...]
    pallas_call x0 -> x3, Pallas kernels: none -> 230 us  [the longest x1 193 us: exchange(): pl.pallas_call(exchange_kernel, out_shape=(jax.ShapeDtypeStruct((64, 2, 4...]
    dot_general x10 -> x0, matrix products: 61.6 us -> none  [the longest x3 24.9 us: block_partial(): jnp.einsum('brd,btd->brt', queried, key_rows, preferred_element_type=jnp....]
    all_to_all x5 -> x0, starting transfers between devices: 45.9 us -> none  [the longest x1 12.1 us: per_device(): lax.all_to_all(send_buffer, 'dec', split_axis=0, concat_axis=0, tiled=True)]
    scatter x2 -> x0, local copies, waits for them, and re-layouts: 15.5 us -> none  [the longest x1 9.12 us: per_device(): jnp.zeros((slot_count, head_count, feature_width), jnp.bfloat16)]
    reduce_sum x7 -> x1, other arithmetic: 15.6 us -> 0.22 us  [per_device(): jnp.sum(jnp.where(pick, page_tokens.reshape(64, 1, 64), 0), axis=2)]
    gather x7 -> x0, local copies, waits for them, and re-layouts: 11.7 us -> none  [the longest x1 6.21 us: per_device(): lax.all_to_all(summed.reshape(sources, slots_here, head_count, out_width)...]
    unnamed x17 -> x21, local copies, waits for them, and re-layouts: 2.04 us -> 9.74 us
  transfers between devices with their start and end apart: 6 -> 0, of which waited for: 3 -> 0; matrix products, arithmetic and copies ran while one was open for 18% -> 0% of each run, Pallas kernels for 0% -> 0%
where the time goes in v1:
time: 247 us; the launch traced here: 243 us
  Pallas kernels  230 us (93%)
  local copies, waits for them, and re-layouts  12.2 us (5%)
    pallas_call x1, Pallas kernels, exchange(): pl.pallas_call(exchange_kernel, out_shape=(jax.ShapeDtypeStruct((64, 2, 4...  193 us
    pallas_call x1, Pallas kernels, local(): pl.pallas_call(local_kernel, grid=(8,), out_shape=jax.ShapeDtypeStruct((6...  33.3 us
    unnamed x21, local copies, waits for them, and re-layouts  9.74 us

profile of v1, /device:TPU:32, one launch (start us, length us, event | category | flops | bytes accessed | tf_op | source)
XLA Modules:
  0.0 242.6 jit_solution(1878829583890988614)
XLA Ops:
  0.0 1.7 copy-done
  1.7 1.3 copy-done.3
  3.1 0.7 copy-done.4
  3.8 0.7 copy-done.6
  4.4 3.5 %shard_map.100 = (bf16[128,32,576]{2,1,0:T(8,128)(2,1)S(1)}, bf16[128,16,576]{2,1,0:T(8,128)(2,1)S(1)}, s32[64]{0:T(128)S(1)}) custom-call(s32[64]{0:T(128)S(1)} %bitcast.10, s32[4096]{0:T(1024)S(1)} %bitcast.9, bf16[64,32,576]{2,1,0:T(8,128)(2,1)S(1)} %copy-done, bf16[64,16,576]{2,1,0:T(8,128)(2,1)S(1)} %copy-done.3), custom_call_target="tpu_custom_call" | custom-call | tf_op jit(solution)/shard_map/pallas_call | solution.py:53
  8.0 0.0 copy-start.1
  8.0 2.4 copy-done.1
  10.3 1.5 copy-done.2
  11.8 0.0 copy-done.7
  11.8 1.4 copy.17
  13.3 193.1 %shard_map.101 = (bf16[64,2,4,16,576]{4,3,2,1,0:T(8,128)(2,1)}, bf16[32,128,128]{2,1,0:T(8,128)(2,1)}, f32[128,128]{1,0:T(8,128)}) custom-call(bf16[8,8,2,32,576]{4,3,2,1,0:T(8,128)(2,1)} %bitcast.7, bf16[1024,576]{1,0:T(8,128)(2,1)} %bitcast.13, bf16[64,2,16,576]{3,2,1,0:T(8,128)(2,1)} %bitcast.8, bf16[32,512,128]{2,1,0:T(8,128)(2,1)} %vu.3), custom_call_target="tpu_custom_call" | custom-call | tf_op jit(solution)/shard_map/pallas_call | solution.py:362
  206.4 0.0 copy-done.5
  206.4 0.1 compare_reduce_fusion
  206.4 0.1 eq.32
  206.5 0.2 reduce_window_sum.11
  206.7 0.1 broadcast_in_dim.25
  206.8 0.1 broadcast_in_dim.28
  206.9 0.2 select_reduce_fusion
  207.1 0.1 copy.15
  207.2 0.7 reshape.41.req
  207.9 0.1 copy.16
  208.0 0.6 reshape.42.length
  208.6 0.7 copy.18.slot
  209.3 33.3 %shard_map.102 = bf16[64,4096]{1,0:T(8,128)(2,1)} custom-call(s32[128]{0:T(128)} %reshape.41.req, s32[128]{0:T(128)} %reshape.42.length, bf16[64,32,576]{2,1,0:T(8,128)(2,1)} %q.1, bf16[64,32,576]{2,1,0:T(8,128)(2,1)} %suffix.1, s32[64]{0:T(128)} %slen.1, bf16[128,64,576]{2,1,0:T(8,128)(2,1)} %bitcast.12, bf16[32,512,128]{2,1,0:T(8,128)(2,1)} %vu.3, ...), custom_call_target="tpu_custom_call" | custom-call | tf_op jit(solution)/shard_map/pallas_call | solution.py:466
  (13 shorter events, 0.0 us)
Async XLA Ops:
  0.0 1.7 copy-start
  1.7 1.3 copy-start.3
  3.1 0.7 copy-start.4
  3.8 0.7 copy-start.6
  4.4 7.4 %copy-start.7 = (bf16[1,1024,576]{1,2,0:T(8,128)(2,1)S(1)}, bf16[1,1024,576]{1,2,0:T(8,128)(2,1)}, u32[]{:S(2)}) copy-start(bf16[1,1024,576]{1,2,0:T(8,128)(2,1)} %param.12) | copy-start | bytes 3538948
  8.0 2.4 copy-start.1
  10.3 1.5 copy-start.2
  13.3 193.1 %copy-start.5 = (s32[4096,1]{0,1:T(1,128)S(1)}, s32[4096,1]{0,1:T(1,128)}, u32[]{:S(2)}) copy-start(s32[4096,1]{0,1:T(1,128)} %param.16) | copy-start | bytes 49156
  13.3 193.5 %copy-start.8 = (s32[4096]{0:T(1024)S(1)}, s32[4096]{0:T(1024)}, u32[]{:S(2)}) copy-start(s32[4096]{0:T(1024)} %param.17) | copy-start | bytes 49156
  13.3 193.5 %copy-start.9 = (s32[4096]{0:T(1024)S(1)}, s32[4096]{0:T(1024)}, u32[]{:S(2)}) copy-start(s32[4096]{0:T(1024)} %param.18) | copy-start | bytes 49156

commit v2 on v1

v2 whole, which is shorter than its diff:
```python
import functools

import jax
import jax.numpy as jnp
from jax import lax
from jax.experimental import pallas as pl
from jax.experimental.pallas import tpu as pltpu
from jax.sharding import PartitionSpec as P

MESH = pl.DeviceIdType.MESH
BF, F32 = jnp.bfloat16, jnp.float32
ANY = pl.BlockSpec(memory_space=pl.ANY)
VM = pl.BlockSpec(memory_space=pltpu.VMEM)
SM = pl.BlockSpec(memory_space=pltpu.SMEM)
DL, DQ = 512, 576
DP = 1152
SCALE = 192.0**-0.5
NEG = -1e30
ORDER = (0, 1, -1, 2, -2, 3, -3, 4)
PLAN = ((0, 1, 2), (3, 4), (5, 6), (7,))
D, Q = 256, 64
PIECE = 64
DQDS = (((1, 0)), ((-1, 0)), ((1, 1)), ((-1, 1)), ((2, 0)), ((2, 1)), ((0, 1)))


def bucket_kernel(
    pref, owner, q_hbm, f_hbm, p_hbm, qs_hbm, ps_hbm, pp_hbm, slot, count, queries, fresh, prefix, qs, ps, pp, sem
):
    dec = lax.axis_index("dec")
    loads = [
        pltpu.make_async_copy(p_hbm, prefix, sem.at[0]),
        pltpu.make_async_copy(f_hbm, fresh, sem.at[1]),
        pltpu.make_async_copy(q_hbm, queries, sem.at[2]),
    ]
    stores = [
        pltpu.make_async_copy(pp, pp_hbm, sem.at[3]),
        pltpu.make_async_copy(ps, ps_hbm, sem.at[4]),
        pltpu.make_async_copy(qs, qs_hbm, sem.at[5]),
    ]
    for c in loads:
        c.start()
    qs[...] = jnp.zeros_like(qs)
    ps[...] = jnp.zeros_like(ps)

    def clear(i, c):
        count[0, i] = 0
        count[1, i] = 0
        return c

    lax.fori_loop(0, 64, clear, 0, unroll=8)
    half = lax.broadcasted_iota(jnp.int32, (16, 128), 1) // 64
    loads[0].wait()
    pp[:, :DL] = prefix[:512, :DL]
    pp[:, DL : 2 * DL] = prefix[512:, :DL]
    pp[:, 2 * DL :] = jnp.concatenate([prefix[:512, DL:], prefix[512:, DL:]], axis=1)
    stores[0].start()

    def put_page(i, c):
        o = owner[dec * 64 + i]
        k = count[1, o]
        count[1, o] = k + 1
        page = fresh[i]
        ps[o, :, pl.ds(pl.multiple_of(k * DL, DL), DL)] = page[:, :DL]
        rotary = page[:, DL:].astype(F32)
        both = jnp.concatenate([rotary, rotary], axis=1)
        ps[o, :, 2 * DL :] = jnp.where(half == k, both, ps[o, :, 2 * DL :].astype(F32)).astype(BF)
        return c

    def put_query(i, c):
        p = pref[i]
        k = count[0, p]
        count[0, p] = k + 1
        to = (p % 8) * 16 + (p // 8) * 2 + k
        qs[to] = queries[i]
        slot[i] = to
        return c

    loads[1].wait()
    lax.fori_loop(0, 64, put_page, 0)
    stores[1].start()
    loads[2].wait()
    lax.fori_loop(0, 64, put_query, 0)
    stores[2].start()
    for c in stores:
        c.wait()


def bucket(pref, owner, queries, fresh, prefix):
    qs, ps, pp, slot = pl.pallas_call(
        bucket_kernel,
        out_shape=(
            jax.ShapeDtypeStruct((128, 32, DQ), BF),
            jax.ShapeDtypeStruct((64, 16, DP), BF),
            jax.ShapeDtypeStruct((512, DP), BF),
            jax.ShapeDtypeStruct((64,), jnp.int32),
        ),
        in_specs=[SM, SM, ANY, ANY, ANY],
        out_specs=(ANY, ANY, ANY, SM),
        scratch_shapes=[
            pltpu.SMEM((2, 64), jnp.int32),
            pltpu.VMEM((64, 32, DQ), BF),
            pltpu.VMEM((64, 16, DQ), BF),
            pltpu.VMEM((1024, DQ), BF),
            pltpu.VMEM((128, 32, DQ), BF),
            pltpu.VMEM((64, 16, DP), BF),
            pltpu.VMEM((512, DP), BF),
            pltpu.SemaphoreType.DMA((6,)),
        ],
        compiler_params=pltpu.CompilerParams(vmem_limit_bytes=60 * 2**20),
    )(pref, owner, queries, fresh, prefix)
    return qs.reshape(8, 8, 2, 32, DQ), ps, pp, slot


def rcopy(src, dst, ss, rs, dev):
    return pltpu.make_async_remote_copy(
        src_ref=src, dst_ref=dst, send_sem=ss, recv_sem=rs, device_id=dev, device_id_type=MESH
    )


def nt(a, b):
    return lax.dot_general(a, b, (((1,), (1,)), ((), ())), preferred_element_type=F32)


def nn(a, b):
    return jnp.dot(a, b, preferred_element_type=F32)


def pad_rotary(q, k):
    r = q[:, DL:]
    zero = jnp.zeros_like(r)
    return jnp.concatenate([zero, r] if k else [r, zero], axis=1)


def exchange_kernel(
    req, length, slen, qs, pf, ps, q_hbm, suffix_hbm, vu_hbm, slot, member, out,
    W, qr, pa, lat, lse, latr, lser, outs, lses, ret, rlse, q, suffix, vu,
    qss, qrs, rss, rrs, pss, prs, xss, xrs, yss, yrs, bss, brs, loc,
):
    pre, dec, rep = lax.axis_index("pre"), lax.axis_index("dec"), lax.axis_index("rep")
    z, y, core = dec // 8, (dec // 2) % 4, dec % 2
    yc = dec % 8
    x = rep * 2 + pre
    g = pre * 2 + rep

    def at_x(v):
        v = v % 4
        return (v % 2, dec, v // 2)

    def g_of(v):
        v = v % 4
        return (v % 2) * 2 + v // 2

    right, left = at_x(x + 1), at_x(x + 3)
    bar = pltpu.get_barrier_semaphore()

    def hello(o, c):
        pl.semaphore_signal(bar, inc=1, device_id=(pre, (dec + o) % 64, rep), device_id_type=MESH)
        return c

    lax.fori_loop(1, 64, hello, 0)
    pl.semaphore_signal(bar, inc=1, device_id=right, device_id_type=MESH)
    pl.semaphore_signal(bar, inc=1, device_id=left, device_id_type=MESH)
    pl.semaphore_wait(bar, 65)

    def start(c):
        c.start()
        return c

    own_q = start(pltpu.make_async_copy(qs.at[yc], qr.at[:, yc], loc.at[0]))
    own_p = start(pltpu.make_async_copy(pf, pa.at[z], loc.at[1]))
    own_w = start(pltpu.make_async_copy(ps.at[dec], W.at[dec, g], loc.at[2]))
    loads = [
        start(pltpu.make_async_copy(q_hbm, q, loc.at[5])),
        start(pltpu.make_async_copy(suffix_hbm, suffix, loc.at[6])),
        start(pltpu.make_async_copy(vu_hbm, vu, loc.at[7])),
    ]

    def peer(dy, dc):
        return ((y + dy + 4) % 4) * 2 + (core + dc) % 2

    def query_send(j, n):
        dy, dc = DQDS[n]
        t = peer(dy, dc)
        part = pl.ds(2 * j, 2)
        return start(rcopy(qs.at[t, part], qr.at[part, yc], qss.at[n], qrs.at[n], (pre, z * 8 + t, rep)))

    def query_wait(n):
        dy, dc = DQDS[n]
        s = peer(-dy, dc)
        return rcopy(qs.at[0], qr.at[:, s], qss.at[n], qrs.at[n], (pre, z * 8 + s, rep))

    def zdev(dz):
        return (pre, ((z + dz + 8) % 8) * 8 + yc, rep)

    def piece(n, last, dirn):
        if n == 0:
            return pl.ds(D + g * Q + dirn * (Q // 2), Q // 2) if last else pl.ds(D + g * Q, Q)
        return pl.ds((n - 1) * PIECE, PIECE)

    def pieces(dirn, t):
        if t < 4:
            return (0, 1, 2, 3, 4)
        return (0, 1, 2) if dirn == 0 else (0, 3, 4)

    rings = {}

    def ring_start(dirn, t, n):
        sgn = 1 - 2 * dirn
        blk = (z - sgn * (t - 1) + 8) % 8
        rows = piece(n, t == 4, dirn)
        src = pf.at[rows] if t == 1 else pa.at[blk, rows]
        rings[dirn, t, n] = start(
            rcopy(src, pa.at[blk, rows], rss.at[dirn, t - 1, n], rrs.at[dirn, t - 1, n], zdev(sgn))
        )

    def page_send(b):
        dz = ORDER[b]

        def one(o, c):
            t = ((z + dz + 8) % 8) * 8 + (yc + o) % 8
            rcopy(ps.at[t], W.at[dec, g], pss.at[b], prs.at[b], (pre, t, rep)).start()
            return c

        lax.fori_loop(1 if dz == 0 else 0, 8, one, 0)

    def batch(b, first=0, count=8):
        return pl.ds(((z - ORDER[b] + 8) % 8) * 8 + first, count)

    def page_wait(b):
        w = W.at[pl.ds(0, 7 if ORDER[b] == 0 else 8), 0]
        c = rcopy(w, w, pss.at[b], prs.at[b], right)
        c.wait_send()
        c.wait_recv()

    xs = {}

    def x_start(b):
        r = W.at[batch(b), g]
        xs[b] = [
            start(rcopy(r, r, xss.at[0, b], xrs.at[0, b], right)),
            start(rcopy(r, r, xss.at[1, b], xrs.at[1, b], left)),
        ]

    def x_forward(b):
        xs[b][0].wait_recv()
        r = W.at[batch(b, 0, 4), g_of(x + 3)]
        xs[b].append(start(rcopy(r, r, xss.at[2, b], xrs.at[2, b], right)))
        xs[b][1].wait_recv()
        r = W.at[batch(b, 4, 4), g_of(x + 1)]
        xs[b].append(start(rcopy(r, r, xss.at[3, b], xrs.at[3, b], left)))

    def x_end(b):
        xs[b][2].wait_recv()
        xs[b][3].wait_recv()

    ys = {}

    def y_start(blk, n):
        r = pa.at[blk, pl.ds(D + g * Q, Q)]
        ys[n] = [
            blk,
            start(rcopy(r, r, yss.at[0, n], yrs.at[0, n], right)),
            start(rcopy(r, r, yss.at[1, n], yrs.at[1, n], left)),
        ]

    def y_forward(n):
        blk = ys[n][0]
        ys[n][1].wait_recv()
        r = pa.at[blk, pl.ds(D + g_of(x + 3) * Q, Q // 2)]
        ys[n].append(start(rcopy(r, r, yss.at[2, n], yrs.at[2, n], right)))
        ys[n][2].wait_recv()
        r = pa.at[blk, pl.ds(D + g_of(x + 1) * Q + Q // 2, Q // 2)]
        ys[n].append(start(rcopy(r, r, yss.at[3, n], yrs.at[3, n], left)))

    def y_end(n):
        ys[n][3].wait_recv()
        ys[n][4].wait_recv()

    def keep(to_lat, to_lse, at, o, l):
        for f in range(4):
            to_lat[f, at, :] = o[:, f * 128 : f * 128 + 128]
        to_lse[at, :] = jnp.broadcast_to(l, (l.shape[0], 128))

    def attend(blk):
        def half(i, c):
            queried = qr[blk, pl.ds(i * 4, 4)].reshape(256, DQ)
            head = queried[:, :DL]
            tail = pa[blk, :, 2 * DL :]
            s0 = nt(head, pa[blk, :, :DL]) + nt(pad_rotary(queried, 0), tail)
            s1 = nt(head, pa[blk, :, DL : 2 * DL]) + nt(pad_rotary(queried, 1), tail)
            top = jnp.maximum(jnp.max(s0, axis=1, keepdims=True), jnp.max(s1, axis=1, keepdims=True))
            w0 = jnp.exp((s0 - top) * SCALE).astype(BF)
            w1 = jnp.exp((s1 - top) * SCALE).astype(BF)
            total = jnp.sum(w0.astype(F32), axis=1, keepdims=True) + jnp.sum(w1.astype(F32), axis=1, keepdims=True)
            o = (nn(w0, pa[blk, :, :DL]) + nn(w1, pa[blk, :, DL : 2 * DL])) / total
            l = top * SCALE + jnp.log(total)
            for n in range(4):
                at = pl.ds(pl.multiple_of((i * 4 + n) * 512 + blk * 64, 64), 64)
                part = slice(n * 64, n * 64 + 64)
                keep(lat, lse, at, o[part], l[part])
            return c

        lax.fori_loop(0, 2, half, 0)

    def masked(s, w_keys, span, lens):
        count = len(lens)
        rows, cols = count * 32, count * span
        r = lax.broadcasted_iota(jnp.int32, (rows, 1), 0) // 32
        limit = jnp.zeros((rows, 1), jnp.int32)
        for n in range(count):
            limit = jnp.where(r == n, lens[n], limit)
        c = lax.broadcasted_iota(jnp.int32, (rows, cols), 1) - r * span
        ok = (c >= 0) & (c < limit)
        s = jnp.where(ok, s * SCALE, NEG)
        m = jnp.max(s, axis=1, keepdims=True)
        w = jnp.where(ok, jnp.exp(s - m), 0.0).astype(BF)
        l = jnp.sum(w.astype(F32), axis=1, keepdims=True)
        l = jnp.where(l > 0.0, l, 1.0)
        return nn(w, w_keys) / l, m + jnp.log(l)

    def resident(i):
        queried = q[pl.ds(i * 8, 8)].reshape(256, DQ)
        keys = suffix[pl.ds(i * 8, 8)].reshape(256, DQ)
        o, l = masked(nt(queried, keys), keys[:, :DL], 32, [slen[i * 8 + n] for n in range(8)])
        keep(latr, lser, pl.ds(pl.multiple_of(i * 256, 256), 256), o, l)

    def residents(i, j):
        def one(n, c):
            resident(n)
            return c

        lax.fori_loop(i, j, one, 0)

    def page_attend(b):
        base = ((z - ORDER[b] + 8) % 8) * 8

        def one(i, c):
            src = base + i * 4
            tail = W[pl.ds(src, 4), :, :, 2 * DL :].reshape(256, 128)
            for k in range(2):
                slots = [(src + n) * 2 + k for n in range(4)]
                queried = jnp.concatenate([q[req[v]] for v in slots], axis=0)
                keys = W[pl.ds(src, 4), :, :, k * DL : k * DL + DL].reshape(256, DL)
                s = nt(queried[:, :DL], keys) + nt(pad_rotary(queried, k), tail)
                o, l = masked(s, keys, 64, [length[v] for v in slots])
                for n in range(4):
                    part = slice(n * 32, n * 32 + 32)
                    keep(lat, lse, pl.ds(pl.multiple_of(slots[n] * 32, 32), 32), o[part], l[part])
            return c

        lax.fori_loop(0, 2, one, 0)

    def gathered(ref, rows):
        return jnp.concatenate([ref[f, rows, :] for f in range(4)], axis=1).astype(BF)

    lane = lax.broadcasted_iota(jnp.int32, (128, 128), 1)

    for n in range(5):
        ring_start(0, 1, n)
        ring_start(1, 1, n)
        if n == 0:
            for b in PLAN[0]:
                page_send(b)
        else:
            for m in range(7):
                query_send(n - 1, m)
    loads[0].wait()
    loads[1].wait()
    for t in range(1, 5):
        residents(2 * t - 2, 2 * t)
        for n in range(5):
            for dirn in (0, 1):
                if n not in pieces(dirn, t):
                    continue
                rings[dirn, t, n].wait_recv()
                if t < 4 and n in pieces(dirn, t + 1):
                    ring_start(dirn, t + 1, n)
                if n == 0 and t < 4:
                    y_start((z - t + 8) % 8 if dirn == 0 else (z + t) % 8, 2 * t - 2 + dirn)
            if t == 4 and n == 0:
                y_start((z + 4) % 8, 6)
        if t < 4:
            for b in PLAN[t]:
                page_send(b)
        if t == 1:
            own_w.wait()
        for b in PLAN[t - 1]:
            page_wait(b)
            x_start(b)
        if t == 4:
            y_forward(6)
        else:
            y_forward(2 * t - 2)
            y_forward(2 * t - 1)
        if t < 4:
            for b in PLAN[t - 1]:
                x_forward(b)
    own_q.wait()
    own_p.wait()
    for n in range(7):
        query_wait(n).wait_recv()
    attend(z)
    y_end(0)
    y_end(1)
    attend((z + 7) % 8)
    attend((z + 1) % 8)
    y_end(2)
    y_end(3)
    attend((z + 6) % 8)
    attend((z + 2) % 8)
    for b in PLAN[3]:
        x_forward(b)
    y_end(4)
    y_end(5)
    attend((z + 5) % 8)
    attend((z + 3) % 8)
    y_end(6)
    attend((z + 4) % 8)
    loads[2].wait()

    def project(h, c):
        rows = pl.ds(h, 128, stride=32)
        outs[h] = nn(gathered(lat, rows), vu[h]).astype(BF)
        return jnp.where(lane == h, lse[rows, :], c)

    lses[...] = lax.fori_loop(0, 32, project, jnp.zeros((128, 128), F32), unroll=2)

    back = []
    for n in range(7):
        dy, dc = DQDS[n]
        t = peer(dy, dc)
        there, here = pl.ds(t * 16, 16), pl.ds(yc * 16, 16)
        dev = (pre, z * 8 + t, rep)
        back.append(start(rcopy(outs.at[:, there], ret.at[:, here], bss.at[0, n], brs.at[0, n], dev)))
        back.append(start(rcopy(lses.at[there], rlse.at[here], bss.at[1, n], brs.at[1, n], dev)))
    here = pl.ds(yc * 16, 16)
    mine = [
        start(pltpu.make_async_copy(outs.at[:, here], ret.at[:, here], loc.at[3])),
        start(pltpu.make_async_copy(lses.at[here], rlse.at[here], loc.at[4])),
    ]

    for b in range(8):
        x_end(b)
        page_attend(b)

    for c in back:
        c.wait()
    for c in mine:
        c.wait()

    def column(h, c):
        return jnp.where(lane == h, lse[pl.ds(h, 128, stride=32), :], c)

    lses[...] = jnp.transpose(lax.fori_loop(0, 32, column, jnp.zeros((128, 128), F32)))
    hot = lax.broadcasted_iota(jnp.int32, (64, 128), 1) == slot[...]
    pick = hot.astype(BF)
    mem = lax.broadcasted_iota(jnp.int32, (64, 128), 0) == member[...]
    plse = jnp.dot(hot.astype(F32), rlse[...], precision=lax.Precision.HIGHEST, preferred_element_type=F32)

    def finish(h, c):
        rows = pl.ds(h, 64, stride=32)
        lp = jnp.sum(jnp.where(lane[:64] == h, plse, 0.0), axis=1, keepdims=True)
        lr = lser[rows, :][:, :1]
        lw = jnp.where(mem, lses[pl.ds(h, 1), :], NEG)
        high = jnp.maximum(jnp.maximum(lp, lr), jnp.max(lw, axis=1, keepdims=True))
        wp, wr = jnp.exp(lp - high), jnp.exp(lr - high)
        ww = jnp.where(mem, jnp.exp(lw - high), 0.0).astype(BF)
        below = wp + wr + jnp.sum(ww.astype(F32), axis=1, keepdims=True)
        v = vu[h]
        paged = nn(ww, nn(gathered(lat, pl.ds(h, 128, stride=32)), v).astype(BF))
        total = wp * nn(pick, ret[h]) + wr * nn(gathered(latr, rows), v) + paged
        out[:, pl.ds(pl.multiple_of(h * 128, 128), 128)] = (total / below).astype(BF)
        return c

    lax.fori_loop(0, 32, finish, 0, unroll=4)

    for n in range(7):
        query_wait(n).wait_send()
        for c in ys[n][1:]:
            c.wait_send()
    for c in rings.values():
        c.wait_send()
    for b in range(8):
        for c in xs[b]:
            c.wait_send()


def exchange(req, length, slen, qs, pf, ps, q, suffix, vu, slot, member):
    S = pltpu.SemaphoreType.DMA
    return pl.pallas_call(
        exchange_kernel,
        out_shape=jax.ShapeDtypeStruct((64, 4096), BF),
        in_specs=[SM, SM, SM] + [ANY] * 6 + [VM, VM],
        out_specs=VM,
        scratch_shapes=[
            pltpu.VMEM((64, 4, 16, DP), BF),
            pltpu.VMEM((8, 8, 2, 32, DQ), BF),
            pltpu.VMEM((8, 512, DP), BF),
            pltpu.VMEM((4, 4096, 128), F32),
            pltpu.VMEM((4096, 128), F32),
            pltpu.VMEM((4, 2048, 128), F32),
            pltpu.VMEM((2048, 128), F32),
            pltpu.VMEM((32, 128, 128), BF),
            pltpu.VMEM((128, 128), F32),
            pltpu.VMEM((32, 128, 128), BF),
            pltpu.VMEM((128, 128), F32),
            pltpu.VMEM((64, 32, DQ), BF),
            pltpu.VMEM((64, 32, DQ), BF),
            pltpu.VMEM((32, DL, 128), BF),
            S((7,)), S((7,)), S((2, 4, 5)), S((2, 4, 5)), S((8,)), S((8,)),
            S((4, 8)), S((4, 8)), S((4, 7)), S((4, 7)), S((2, 7)), S((2, 7)), S((8,)),
        ],
        compiler_params=pltpu.CompilerParams(
            collective_id=0, has_side_effects=True, vmem_limit_bytes=60 * 2**20
        ),
    )(req, length, slen, qs, pf, ps, q, suffix, vu, slot, member)


def per_device(
    queries, prefix_of, prefix_cache, suffix_cache, suffix_len, fresh_pages,
    page_owner, page_request, page_tokens, value_up,
):
    dec = lax.axis_index("dec")
    qs, ps, pp, slot = bucket(prefix_of[:, 0], page_owner[:, 0], queries, fresh_pages, prefix_cache[0])

    mine = page_owner[:, 0].reshape(64, 64) == dec
    nth = jnp.cumsum(mine.astype(jnp.int32), axis=1)
    pick = mine[:, None, :] & (nth[:, None, :] == jnp.arange(1, 3)[None, :, None])
    req = jnp.sum(jnp.where(pick, page_request.reshape(64, 1, 64), 0), axis=2).reshape(128)
    length = jnp.sum(jnp.where(pick, page_tokens.reshape(64, 1, 64), 0), axis=2).reshape(128)
    member = jnp.where(length > 0, req, -1).reshape(1, 128)
    return exchange(
        req, length, suffix_len, qs, pp, ps, queries, suffix_cache, value_up,
        slot.reshape(64, 1), member,
    )


def solution(mesh):
    heads = ("pre", "rep")
    placed = (
        P("dec", heads, None),
        P("dec", None),
        P("dec", None, None),
        P("dec", None, None),
        P("dec"),
        P("dec", heads, None),
        P(),
        P(),
        P(),
        P(heads, None, None),
    )
    return jax.shard_map(
        per_device, mesh=mesh, in_specs=placed, out_specs=P("dec", heads), check_vma=False
    )
```

time: 247 us -> 223 us (0.903); the launches traced: 243 us -> 222 us
  Pallas kernels: 230 us -> 211 us
  local copies, waits for them, and re-layouts: 12.2 us -> 9.58 us
    pallas_call x2 -> x1, Pallas kernels: 226 us -> 200 us  [exchange(): pl.pallas_call(exchange_kernel, out_shape=jax.ShapeDtypeStruct((64, 4096)...]
    pallas_call x1, Pallas kernels: 3.52 us -> 11.3 us  [bucket(): pl.pallas_call(bucket_kernel, out_shape=(jax.ShapeDtypeStruct((128, 32, D...]
    unnamed x21 -> x2, local copies, waits for them, and re-layouts: 9.74 us -> 4.33 us
where the time goes in v2:
time: 223 us; the launch traced here: 222 us
  Pallas kernels  211 us (95%)
  local copies, waits for them, and re-layouts  9.58 us (4%)
    pallas_call x1, Pallas kernels, exchange(): pl.pallas_call(exchange_kernel, out_shape=jax.ShapeDtypeStruct((64, 4096)...  200 us
    pallas_call x1, Pallas kernels, bucket(): pl.pallas_call(bucket_kernel, out_shape=(jax.ShapeDtypeStruct((128, 32, D...  11.3 us

profile of v2, /device:TPU:32, one launch (start us, length us, event | category | flops | bytes accessed | tf_op | source)
XLA Modules:
  0.0 222.3 jit_solution(6608286140906349959)
XLA Ops:
  0.0 0.8 compare_reduce_fusion
  0.8 0.1 eq.32
  0.9 0.2 reduce_window_sum.11
  1.1 0.8 broadcast_in_dim.29
  1.9 0.8 broadcast_in_dim.32
  2.7 0.2 select_reduce_fusion
  2.9 0.1 copy.16
  3.0 0.7 reshape.61.length
  3.7 0.1 copy.15
  3.8 0.6 reshape.60.req
  4.4 0.1 copy.18
  4.5 0.7 select_n.24.member
  5.2 2.5 %copy.17 = bf16[1,1024,576]{2,1,0:T(8,128)(2,1)} copy(bf16[1,1024,576]{1,2,0:T(8,128)(2,1)} %param.12) | data formatting | bytes 2359296 | tf_op args[2]
  7.6 11.3 %shard_map.100 = (bf16[128,32,576]{2,1,0:T(8,128)(2,1)}, bf16[64,16,1152]{2,1,0:T(8,128)(2,1)}, bf16[512,1152]{1,0:T(8,128)(2,1)}, s32[64]{0:T(128)}) custom-call(s32[64]{0:T(128)} %bitcast.9, s32[4096]{0:T(1024)} %bitcast.7, bf16[64,32,576]{2,1,0:T(8,128)(2,1)} %q_hbm.3, bf16[64,16,576]{2,1,0:T(8,128)(2,1)} %f_hbm.1, bf16[1024,576]{1,0:T(8,128)(2,1)} %bitcast.6), custom_call_target="tpu_custom_call" | custom-call | tf_op jit(solution)/shard_map/pallas_call | solution.py:89
  19.0 1.3 copy.19.slot
  20.3 200.1 %shard_map.101 = bf16[64,4096]{1,0:T(8,128)(2,1)} custom-call(s32[128]{0:T(128)} %reshape.60.req, s32[128]{0:T(128)} %reshape.61.length, s32[64]{0:T(128)} %slen.1, bf16[8,8,2,32,576]{4,3,2,1,0:T(8,128)(2,1)} %bitcast.5, bf16[512,1152]{1,0:T(8,128)(2,1)} %get-tuple-element.10.pf, bf16[64,16,1152]{2,1,0:T(8,128)(2,1)} %get-tuple-element.11.ps, ...), custom_call_target="tpu_custom_call" | custom-call | tf_op jit(solution)/shard_map/pallas_call | solution.py:490
  220.4 1.9 copy.21
  (3 shorter events, 0.0 us)

commit v3 on v2

--- a/solution.py
+++ b/solution.py
@@ -367,7 +367,22 @@
     loads[0].wait()
     loads[1].wait()
     for t in range(1, 5):
-        residents(2 * t - 2, 2 * t)
+        if t < 3:
+            residents(4 * t - 4, 4 * t)
+        if t == 3:
+            own_q.wait()
+            own_p.wait()
+            for n in range(7):
+                query_wait(n).wait_recv()
+            attend(z)
+            y_end(0)
+            y_end(1)
+            attend((z + 7) % 8)
+            attend((z + 1) % 8)
+            y_end(2)
+            y_end(3)
+            attend((z + 6) % 8)
+            attend((z + 2) % 8)
         for n in range(5):
             for dirn in (0, 1):
                 if n not in pieces(dirn, t):
@@ -395,25 +410,12 @@
         if t < 4:
             for b in PLAN[t - 1]:
                 x_forward(b)
-    own_q.wait()
-    own_p.wait()
-    for n in range(7):
-        query_wait(n).wait_recv()
-    attend(z)
-    y_end(0)
-    y_end(1)
-    attend((z + 7) % 8)
-    attend((z + 1) % 8)
-    y_end(2)
-    y_end(3)
-    attend((z + 6) % 8)
-    attend((z + 2) % 8)
-    for b in PLAN[3]:
-        x_forward(b)
     y_end(4)
     y_end(5)
     attend((z + 5) % 8)
     attend((z + 3) % 8)
+    for b in PLAN[3]:
+        x_forward(b)
     y_end(6)
     attend((z + 4) % 8)
     loads[2].wait()
@@ -451,7 +453,7 @@
     def column(h, c):
         return jnp.where(lane == h, lse[pl.ds(h, 128, stride=32), :], c)
 
-    lses[...] = jnp.transpose(lax.fori_loop(0, 32, column, jnp.zeros((128, 128), F32)))
+    lses[...] = jnp.transpose(lax.fori_loop(0, 32, column, jnp.zeros((128, 128), F32), unroll=8))
     hot = lax.broadcasted_iota(jnp.int32, (64, 128), 1) == slot[...]
     pick = hot.astype(BF)
     mem = lax.broadcasted_iota(jnp.int32, (64, 128), 0) == member[...]

time: 223 us -> 218 us (0.978)
  Pallas kernels: 211 us -> 207 us
    pallas_call x1, Pallas kernels: 200 us -> 196 us  [exchange(): pl.pallas_call(exchange_kernel, out_shape=jax.ShapeDtypeStruct((64, 4096)...]
where the time goes in v3:
time: 218 us
  Pallas kernels  207 us (95%)
  local copies, waits for them, and re-layouts  9.58 us (4%)
    pallas_call x1, Pallas kernels, exchange(): pl.pallas_call(exchange_kernel, out_shape=jax.ShapeDtypeStruct((64, 4096)...  196 us
    pallas_call x1, Pallas kernels, bucket(): pl.pallas_call(bucket_kernel, out_shape=(jax.ShapeDtypeStruct((128, 32, D...  11.3 us

profile of v3, /device:TPU:32, one launch (start us, length us, event | category | flops | bytes accessed | tf_op | source)
XLA Modules:
  0.0 217.8 jit_solution(16336895502283024272)
XLA Ops:
  0.0 0.8 compare_reduce_fusion
  0.8 0.1 eq.32
  0.9 0.2 reduce_window_sum.11
  1.1 0.8 broadcast_in_dim.29
  1.9 0.8 broadcast_in_dim.32
  2.7 0.2 select_reduce_fusion
  2.9 0.1 copy.16
  3.0 0.7 reshape.61.length
  3.7 0.1 copy.15
  3.8 0.6 reshape.60.req
  4.4 0.1 copy.18
  4.5 0.7 select_n.24.member
  5.2 2.5 %copy.17 = bf16[1,1024,576]{2,1,0:T(8,128)(2,1)} copy(bf16[1,1024,576]{1,2,0:T(8,128)(2,1)} %param.12) | data formatting | bytes 2359296 | tf_op args[2]
  7.6 11.3 %shard_map.100 = (bf16[128,32,576]{2,1,0:T(8,128)(2,1)}, bf16[64,16,1152]{2,1,0:T(8,128)(2,1)}, bf16[512,1152]{1,0:T(8,128)(2,1)}, s32[64]{0:T(128)}) custom-call(s32[64]{0:T(128)} %bitcast.9, s32[4096]{0:T(1024)} %bitcast.7, bf16[64,32,576]{2,1,0:T(8,128)(2,1)} %q_hbm.3, bf16[64,16,576]{2,1,0:T(8,128)(2,1)} %f_hbm.1, bf16[1024,576]{1,0:T(8,128)(2,1)} %bitcast.6), custom_call_target="tpu_custom_call" | custom-call | tf_op jit(solution)/shard_map/pallas_call | solution.py:89
  19.0 1.3 copy.19.slot
  20.3 195.6 %shard_map.101 = bf16[64,4096]{1,0:T(8,128)(2,1)} custom-call(s32[128]{0:T(128)} %reshape.60.req, s32[128]{0:T(128)} %reshape.61.length, s32[64]{0:T(128)} %slen.1, bf16[8,8,2,32,576]{4,3,2,1,0:T(8,128)(2,1)} %bitcast.5, bf16[512,1152]{1,0:T(8,128)(2,1)} %get-tuple-element.10.pf, bf16[64,16,1152]{2,1,0:T(8,128)(2,1)} %get-tuple-element.11.ps, ...), custom_call_target="tpu_custom_call" | custom-call | tf_op jit(solution)/shard_map/pallas_call | solution.py:492
  215.9 1.9 copy.21
  (3 shorter events, 0.0 us)

commit v4 on v3

--- a/solution.py
+++ b/solution.py
@@ -411,11 +411,11 @@
             for b in PLAN[t - 1]:
                 x_forward(b)
     y_end(4)
-    y_end(5)
     attend((z + 5) % 8)
-    attend((z + 3) % 8)
     for b in PLAN[3]:
         x_forward(b)
+    y_end(5)
+    attend((z + 3) % 8)
     y_end(6)
     attend((z + 4) % 8)
     loads[2].wait()

time: 218 us -> 219 us (level)
  no operation moved by 1% of the time
where the time goes in v4:
time: 219 us; the launch traced here: 218 us
  Pallas kernels  208 us (95%)
  local copies, waits for them, and re-layouts  9.58 us (4%)
    pallas_call x1, Pallas kernels, exchange(): pl.pallas_call(exchange_kernel, out_shape=jax.ShapeDtypeStruct((64, 4096)...  196 us
    pallas_call x1, Pallas kernels, bucket(): pl.pallas_call(bucket_kernel, out_shape=(jax.ShapeDtypeStruct((128, 32, D...  11.3 us

profile of v4, /device:TPU:32, one launch (start us, length us, event | category | flops | bytes accessed | tf_op | source)
XLA Modules:
  0.0 218.5 jit_solution(3284970923785428557)
XLA Ops:
  0.0 0.8 compare_reduce_fusion
  0.8 0.1 eq.32
  0.9 0.2 reduce_window_sum.11
  1.1 0.8 broadcast_in_dim.29
  1.9 0.8 broadcast_in_dim.32
  2.7 0.2 select_reduce_fusion
  2.9 0.1 copy.16
  3.0 0.7 reshape.61.length
  3.7 0.1 copy.15
  3.8 0.6 reshape.60.req
  4.4 0.1 copy.18
  4.5 0.7 select_n.24.member
  5.2 2.5 %copy.17 = bf16[1,1024,576]{2,1,0:T(8,128)(2,1)} copy(bf16[1,1024,576]{1,2,0:T(8,128)(2,1)} %param.12) | data formatting | bytes 2359296 | tf_op args[2]
  7.6 11.3 %shard_map.100 = (bf16[128,32,576]{2,1,0:T(8,128)(2,1)}, bf16[64,16,1152]{2,1,0:T(8,128)(2,1)}, bf16[512,1152]{1,0:T(8,128)(2,1)}, s32[64]{0:T(128)}) custom-call(s32[64]{0:T(128)} %bitcast.9, s32[4096]{0:T(1024)} %bitcast.7, bf16[64,32,576]{2,1,0:T(8,128)(2,1)} %q_hbm.3, bf16[64,16,576]{2,1,0:T(8,128)(2,1)} %f_hbm.1, bf16[1024,576]{1,0:T(8,128)(2,1)} %bitcast.6), custom_call_target="tpu_custom_call" | custom-call | tf_op jit(solution)/shard_map/pallas_call | solution.py:89
  19.0 1.3 copy.19.slot
  20.3 196.3 %shard_map.101 = bf16[64,4096]{1,0:T(8,128)(2,1)} custom-call(s32[128]{0:T(128)} %reshape.60.req, s32[128]{0:T(128)} %reshape.61.length, s32[64]{0:T(128)} %slen.1, bf16[8,8,2,32,576]{4,3,2,1,0:T(8,128)(2,1)} %bitcast.5, bf16[512,1152]{1,0:T(8,128)(2,1)} %get-tuple-element.10.pf, bf16[64,16,1152]{2,1,0:T(8,128)(2,1)} %get-tuple-element.11.ps, ...), custom_call_target="tpu_custom_call" | custom-call | tf_op jit(solution)/shard_map/pallas_call | solution.py:492
  216.6 1.9 copy.21
  (3 shorter events, 0.0 us)
